TPU v7x, 32 devices: a whole 2x2x4 slice. The times are simulated.
32 devices in a mesh: redist: 16 (over z, y, x), contract: 2 (over core).
Axes of the slice: x: 2, y: 2, z: 4, core: 2. Of those that a mesh axis runs over, the one named last changes fastest.
Arguments:
- amps: float32 [6400, 128, 128], P('redist', None, 'contract'), may hold values from -6 to 6
- integrals: float32 [80, 128, 16, 128], P(None, 'contract'), may hold values from -0.3125 to 0.3125
- occ_irrep: int32 [80], replicated, may hold values from 0 to 7
- block_sizes: int32 [8], replicated, may hold values from 1 to 128, 800 in all
- slot_order: int32 [128], replicated, may hold values from 0 to 127, each once
- occ_energy: float32 [80], replicated, may hold values from -3 to -0.5
- vir_energy: float32 [8, 128], replicated, may hold values from 0.3 to 3
Outputs:
- update: float32 [80, 128, 16, 128], P(None, 'redist', None, 'contract')
Inputs may be any that keep to these rules, and one draw needn't show every extreme that they name: `block_sizes`: block sizes of the 8 occupied irreps sum to 800; the largest is 128. `slot_order`: each slot appears once.
All inputs are finite; a program needn't handle non-finite values.
Results may differ from a plain program's by a relative error of at most 0.00007.
Values sent between devices are 32-bit elements; how exact they have to be, the bound alone decides.
A program may use at most 192 MiB of HBM per device.

v0:
```python
import jax
import jax.numpy as jnp
from jax import lax
from jax.sharding import PartitionSpec as P


def per_device(amps, integrals, occ_irrep, block_sizes, slot_order, occ_energy, vir_energy):
    redist_count = lax.axis_size("redist")
    occ_total = occ_irrep.shape[0]
    slab = integrals.shape[2]
    share = integrals.shape[1]
    irrep_total = vir_energy.shape[0]
    slot_total = vir_energy.shape[1]
    slot_dev = slot_total // redist_count
    labels = jnp.arange(irrep_total, dtype=jnp.int32)
    hits = occ_irrep[:, None] == labels[None, :]
    occ_limit = jnp.sum(jnp.where(hits, block_sizes[None, :], 0), axis=1)
    ordered = jnp.take(amps, slot_order, axis=1)
    moved = lax.all_to_all(ordered, "redist", split_axis=1, concat_axis=0, tiled=True)
    blocks = moved.reshape(occ_total, occ_total, slot_dev, share)
    col_first = lax.axis_index("contract") * share
    col_ids = col_first + jnp.arange(share, dtype=jnp.int32)
    keep_kc = col_ids[None, :] < occ_limit[:, None]
    masked = jnp.where(keep_kc[:, None, None, :], blocks, jnp.zeros((), blocks.dtype))
    summed = lax.psum_scatter(
        jnp.einsum(
            "kiac,kcjb->biaj",
            masked,
            integrals,
            precision=lax.Precision.HIGHEST,
            preferred_element_type=jnp.float32,
        ),
        "contract",
        scatter_dimension=0,
        tiled=True,
    )
    cycle = jnp.transpose(summed, (1, 2, 3, 0))
    my_slots = lax.dynamic_slice_in_dim(
        slot_order, lax.axis_index("redist") * slot_dev, slot_dev, 0
    )
    vir_rows = jnp.take(vir_energy, my_slots, axis=1)
    row_energy = jnp.sum(
        jnp.where(hits[:, :, None], vir_rows[None, :, :], jnp.zeros((), vir_rows.dtype)), axis=1
    )
    vir_cols = lax.dynamic_slice_in_dim(vir_energy, col_first, share, 1)
    col_energy = jnp.sum(
        jnp.where(hits[:slab, :, None], vir_cols[None, :, :], jnp.zeros((), vir_cols.dtype)), axis=1
    )
    denom = (
        row_energy[:, :, None, None]
        + col_energy[None, None, :, :]
        - occ_energy[:, None, None, None]
        - occ_energy[:slab][None, None, :, None]
    )
    keep_row = my_slots[None, :] < occ_limit[:, None]
    keep_col = col_ids[None, :] < occ_limit[:slab][:, None]
    keep = keep_row[:, :, None, None] & keep_col[None, None, :, :]
    return jnp.where(keep, cycle / denom, jnp.zeros((), cycle.dtype))


def solution(mesh):
    placed = (
        P("redist", None, "contract"),
        P(None, "contract", None, None),
        P(),
        P(),
        P(),
        P(),
        P(),
    )
    return jax.shard_map(
        per_device,
        mesh=mesh,
        in_specs=placed,
        out_specs=P(None, "redist", None, "contract"),
        check_vma=False,
    )
```

profile of v0, /device:TPU:4, one launch (start us, length us, event | category | flops | bytes accessed | tf_op | source)
XLA Modules:
  0.0 642.0 jit_solution(6843587188581898289)
XLA Ops:
  6.5 0.7 compare_select_fusion.1
  7.2 0.7 compare_and_fusion.1
  7.9 17.3 %copy.27 = f32[400,128,64]{0,2,1:T(8,128)} copy(f32[400,128,64]{1,2,0:T(8,128)} %param.7) | data formatting | bytes 26214400 | tf_op args[0]
  25.2 15.6 %gather_fusion = f32[128,400,64]{1,2,0:T(8,128)} fusion(f32[400,128,64]{0,2,1:T(8,128)} %copy.27, s32[1024]{0:T(1024)S(1)} %pad_clamp_fusion.1), kind=kCustom, calls=%fused_computation | custom fusion | bytes 26214912 | tf_op jit(solution)/shard_map/jit(_take)/gather | solution.py:18
  40.8 12.1 %select_bitcast_fusion = f32[400,128,64]{0,2,1:T(8,128)} fusion(f32[128,400,64]{1,2,0:T(8,128)} %gather_fusion, pred[128]{0:T(512)(128)(4,1)S(1)} %compare_and_fusion.1), kind=kLoop, calls=%fused_computation.7 | loop fusion | flops 3276800 | bytes 26214528 | tf_op jit(solution)/shard_map/jit(_take)/select_n | solution.py:18
  52.9 0.0 copy-start.3
  52.9 0.0 copy-start.4
  52.9 7.4 %all-to-all-start = ((f32[400,128,64]{0,2,1:T(8,128)}), f32[400,128,64]{0,2,1:T(8,128)}, u32[]{:S(2)}, u32[]{:S(2)}) async-start(f32[400,128,64]{0,2,1:T(8,128)} %select_bitcast_fusion), calls=%async_computation | async-start | bytes 33554432 | tf_op jit(solution)/shard_map/all_to_all | solution.py:19
  60.4 0.0 reduce-scatter.2.cloned.1.call-start
  60.4 0.0 copy-done.3
  60.4 0.0 copy-done.4
  60.4 0.1 select_reduce_fusion.2
  60.5 0.1 broadcast_compare_fusion
  60.6 336.2 %all-to-all-done = f32[400,128,64]{0,2,1:T(8,128)} async-done(((f32[400,128,64]{0,2,1:T(8,128)}), f32[400,128,64]{0,2,1:T(8,128)}, u32[]{:S(2)}, u32[]{:S(2)}) %all-to-all-start) | async-done | bytes 13107232 | tf_op jit(solution)/shard_map/all_to_all | solution.py:19
  396.8 17.8 %copy.28 = f32[16,400,8,64]{1,0,3,2:T(8,128)} copy(f32[16,400,8,64]{1,3,2,0:T(8,128)} %bitcast.2) | data formatting | bytes 26214400 | tf_op jit(solution)/shard_map/all_to_all | solution.py:19
  414.6 24.2 %reshape.136 = f32[80,80,8,64]{1,0,3,2:T(8,128)} reshape(f32[16,400,8,64]{1,0,3,2:T(8,128)} %copy.28) | data formatting | bytes 26214400 | tf_op jit(solution)/shard_map/reshape | solution.py:20
  438.8 117.6 %fusion.8 = f32[128,80,8,16]{0,1,3,2:T(8,128)} fusion(f32[80,64,16,128]{3,2,1,0:T(8,128)} %param.8, f32[80,80,8,64]{1,0,3,2:T(8,128)} %reshape.136, pred[80,64]{0,1:T(8,128)(4,1)S(1)} %broadcast_compare_fusion), kind=kOutput, calls=%fused_computation.12 | convolution fusion | flops 80533913600 | bytes 60298240 | tf_op jit(solution)/shard_map/kiac,kcjb->biaj/dot_general | solution.py:26
  556.5 0.0 copy-start
  556.5 0.0 copy-start.2
  556.5 0.0 copy-start.1
  556.5 8.1 %copy.31 = f32[128,80,8,16]{1,3,2,0:T(8,128)} copy(f32[128,80,8,16]{0,1,3,2:T(8,128)} %fusion.8) | data formatting | bytes 10485760 | tf_op jit(solution)/shard_map/kiac,kcjb->biaj/transpose | solution.py:26
  564.6 0.0 reduce-scatter.2.cloned.1.call-update
  564.6 0.1 copy.34
  564.7 0.0 copy-done
  564.7 0.1 copy.32
  564.8 0.1 constant_dynamic-slice_fusion
  564.9 0.1 select_reduce_fusion
  565.0 0.1 copy.35
  565.1 0.0 copy-done.2
  565.1 0.1 compare_and_fusion
  565.2 0.6 gather_fusion.1
  565.7 0.1 select_bitcast_fusion.1
  565.8 0.1 copy.33
  565.9 0.1 select_reduce_fusion.1
  566.0 0.1 broadcast_compare_fusion.2
  566.0 0.1 broadcast_compare_fusion.1
  566.1 61.7 %reduce-scatter.2.cloned.1.call-done = f32[64,80,8,16]{1,3,2,0:T(8,128)} async-done(((f32[128,80,8,16]{1,3,2,0:T(8,128)}), f32[64,80,8,16]{1,3,2,0:T(8,128)}) %reduce-scatter.2.cloned.1.call-update) | async-done | bytes 2621456 | tf_op jit(solution)/shard_map/reduce_scatter | solution.py:25
  627.8 0.0 copy-done.1
  627.8 2.9 fusion.7
  630.7 4.4 copy.36
  (5 shorter events, 0.0 us)
Async XLA Ops:
  52.9 7.5 %copy-start.3 = (s32[8]{0:T(128)S(1)}, s32[8]{0:T(128)}, u32[]{:S(2)}) copy-start(s32[8]{0:T(128)} %param.10) | copy-start | bytes 100
  52.9 7.5 %copy-start.4 = (s32[80]{0:T(128)S(1)}, s32[80]{0:T(128)}, u32[]{:S(2)}) copy-start(s32[80]{0:T(128)} %param.9) | copy-start | bytes 964
  52.9 343.9 %all-to-all-start = ((f32[400,128,64]{0,2,1:T(8,128)}), f32[400,128,64]{0,2,1:T(8,128)}, u32[]{:S(2)}, u32[]{:S(2)}) async-start(f32[400,128,64]{0,2,1:T(8,128)} %select_bitcast_fusion), calls=%async_computation | async-start | bytes 33554432 | tf_op jit(solution)/shard_map/all_to_all | solution.py:19
  60.4 567.4 %reduce-scatter.2.cloned.1.call-start = ((), (), s32[]{:S(2)}) async-start(), calls=%async_computation.2 | async-start | bytes 12582912 | tf_op jit(solution)/shard_map/reduce_scatter | solution.py:25
  556.5 8.2 %copy-start = (f32[8,128]{1,0:T(8,128)S(1)}, f32[8,128]{1,0:T(8,128)}, u32[]{:S(2)}) copy-start(f32[8,128]{1,0:T(8,128)} %param.13) | copy-start | bytes 12292
  556.5 8.6 %copy-start.2 = (s32[128]{0:T(128)S(1)}, s32[128]{0:T(128)}, u32[]{:S(2)}) copy-start(s32[128]{0:T(128)} %param.11) | copy-start | bytes 1540
  556.5 71.3 %copy-start.1 = (f32[80]{0:T(128)S(1)}, f32[80]{0:T(128)}, u32[]{:S(2)}) copy-start(f32[80]{0:T(128)} %param.12) | copy-start | bytes 964
Sparse Core Ops, SparseCore 0:
  564.7 63.0 reduce-scatter.1
where the time goes:
time: 644 us; the launch traced here: 642 us
  waiting for transfers between devices  398 us (62%)
  matrix products  118 us (18%)
  local copies, waits for them, and re-layouts  88.5 us (14%)
  other arithmetic  17 us (3%)
  between operations  13.5 us (2%)
  starting transfers between devices  7.45 us (1%)
    all_to_all x1, waiting for transfers between devices, per_device(): lax.all_to_all(ordered, 'redist', split_axis=1, concat_axis=0, tiled=True)  336 us
    dot_general x1, matrix products, per_device(): jnp.einsum('kiac,kcjb->biaj', masked, integrals, precision=lax.Precision....  118 us
    reduce_scatter x1, waiting for transfers between devices, per_device(): lax.psum_scatter(jnp.einsum('kiac,kcjb->biaj', masked, integrals, precisi...  61.7 us
    reshape x1, local copies, waits for them, and re-layouts, per_device(): blocks = moved.reshape(occ_total, occ_total, slot_dev, share)  24.2 us
    all_to_all x1, local copies, waits for them, and re-layouts, per_device(): lax.all_to_all(ordered, 'redist', split_axis=1, concat_axis=0, tiled=True)  17.8 us
    unnamed x12, local copies, waits for them, and re-layouts  17.4 us
    gather x1, local copies, waits for them, and re-layouts, per_device(): ordered = jnp.take(amps, slot_order, axis=1)  15.6 us
  transfers between devices with their start and end apart: 2, of which 2 were waited for; matrix products, arithmetic and copies ran while one was open for 0% of the time, Pallas kernels for 0%

commit v1 on v0

--- a/solution.py
+++ b/solution.py
@@ -1,25 +1,267 @@
+import functools
 import jax
 import jax.numpy as jnp
 from jax import lax
+from jax.experimental import pallas as pl
+from jax.experimental.pallas import tpu as pltpu
 from jax.sharding import PartitionSpec as P
 
-
-def per_device(amps, integrals, occ_irrep, block_sizes, slot_order, occ_energy, vir_energy):
+MESH = pl.DeviceIdType.MESH
+PLANE = 4
+LAYERS = 4
+
+
+def split(x):
+    hi = x.astype(jnp.bfloat16)
+    return hi, (x - hi.astype(jnp.float32)).astype(jnp.bfloat16)
+
+
+def regroup_kernel(x_ref, first_ref, second_ref, out_ref):
+    pair, _, group, share, lanes = x_ref.shape
+    rows = pair * share
+    inner = []
+    for high in range(PLANE):
+        wide = jnp.concatenate(
+            [x_ref[:, 0, high * LAYERS + low].reshape(rows, lanes) for low in range(LAYERS)], axis=1
+        )
+        both = jnp.concatenate(split(wide), axis=0)
+        inner.append(
+            jnp.dot(both, first_ref[...], preferred_element_type=jnp.float32).astype(jnp.bfloat16)
+        )
+    for layer in range(LAYERS):
+        wide = jnp.concatenate([one[:, layer * lanes:(layer + 1) * lanes] for one in inner], axis=1)
+        picked = jnp.dot(wide, second_ref[...], preferred_element_type=jnp.float32)
+        picked = picked[:rows] + picked[rows:]
+        for mate in range(PLANE):
+            out_ref[mate, 0, layer] = picked[:, mate * lanes:(mate + 1) * lanes]
+
+
+def cycle_kernel(
+    a_ref, hi_ref, lo_ref, out_ref,
+    got, x_hi, x_lo, part, both, near, far,
+    own_sem, swap_send, swap_recv, core_send, core_recv, near_send, near_recv, far_send, far_recv,
+):
+    groups = a_ref.shape[1]
+    rows = a_ref.shape[3]
+    lanes = a_ref.shape[4]
+    full = hi_ref.shape[0]
+    half = full // 2
+    me = lax.axis_index("redist")
+    core = lax.axis_index("contract")
+    layer, mate = me // PLANE, me % PLANE
+    mate_y, mate_x = mate // 2, mate % 2
+    mates = [((mate_y + d // 2) % 2) * 2 + (mate_x + d % 2) % 2 for d in range(PLANE)]
+    beside = layer + 1 - 2 * (layer % 2)
+    across = (layer + 2) % LAYERS
+    beyond = (beside + 2) % LAYERS
+    other = 1 - core
+
+    barrier = pltpu.get_barrier_semaphore()
+    partners = [(layer * PLANE + mates[d], core) for d in range(1, PLANE)]
+    partners += [(me, other), (beside * PLANE + mate, core), (across * PLANE + mate, core)]
+    for partner in partners:
+        pl.semaphore_signal(barrier, inc=1, device_id=partner, device_id_type=MESH)
+    pl.semaphore_wait(barrier, len(partners))
+
+    def own(g):
+        return pltpu.make_async_copy(a_ref.at[mate, g], got.at[g, 0], own_sem.at[g])
+
+    def remote(src, dst, send, recv, device):
+        return pltpu.make_async_remote_copy(
+            src_ref=src, dst_ref=dst, send_sem=send, recv_sem=recv,
+            device_id=device, device_id_type=MESH,
+        )
+
+    def swap(g, d):
+        return remote(a_ref.at[mates[d], g], got.at[g, d], swap_send.at[g, d - 1],
+                      swap_recv.at[g, d - 1], (layer * PLANE + mates[d], core))
+
+    def cores(g):
+        return remote(part.at[g % 2, :, pl.ds(other * half, half), :], both.at[g],
+                      core_send.at[g], core_recv.at[g], (me, other))
+
+    def nearby(g, n):
+        block = beyond if n else beside
+        return remote(both.at[g, block], near.at[g, n], near_send.at[g, n],
+                      near_recv.at[g, n], (beside * PLANE + mate, core))
+
+    def away(g):
+        return remote(both.at[g, across], far.at[g], far_send.at[g], far_recv.at[g],
+                      (across * PLANE + mate, core))
+
+    def begin(g):
+        for d in (3, 1, 2):
+            swap(g, d).start()
+        own(g).start()
+
+    def multiply(g):
+        for d in range(PLANE):
+            def cast(b, carry, d=d):
+                at = pl.ds(d * rows, rows)
+                hi, lo = split(got[g, d, b])
+                x_hi[b, at, :] = hi
+                x_lo[b, at, :] = lo
+                return carry
+            lax.fori_loop(0, LAYERS, cast, 0)
+        tile = full // 8
+
+        def step(m, carry):
+            at = pl.ds(pl.multiple_of(m * tile, tile), tile)
+            w_hi, w_lo = hi_ref[at, :], lo_ref[at, :]
+            for b in range(0, LAYERS, 2):
+                xh = jnp.concatenate([x_hi[b], x_hi[b + 1]], axis=1)
+                xl = jnp.concatenate([x_lo[b], x_lo[b + 1]], axis=1)
+                total = jnp.dot(w_hi, xh, preferred_element_type=jnp.float32)
+                total += jnp.dot(w_hi, xl, preferred_element_type=jnp.float32)
+                total += jnp.dot(w_lo, xh, preferred_element_type=jnp.float32)
+                part[g % 2, b, at, :] = total[:, :lanes]
+                part[g % 2, b + 1, at, :] = total[:, lanes:]
+            return carry
+        lax.fori_loop(0, 8, step, 0)
+
+    begin(0)
+    if groups > 1:
+        begin(1)
+    for g in range(groups + 1):
+        if g < groups:
+            own(g).wait()
+            for d in (1, 2, 3):
+                swap(g, d).wait_recv()
+            if g + 2 < groups:
+                begin(g + 2)
+            if g >= 2:
+                cores(g - 2).wait_send()
+            multiply(g)
+            cores(g).start()
+        if g >= 1:
+            nearby(g - 1, 1).wait_recv()
+            both[g - 1, across] = both[g - 1, across] + near[g - 1, 1]
+            away(g - 1).start()
+        if g < groups:
+            cores(g).wait_recv()
+
+            def add(b, carry, g=g):
+                at = pl.ds(pl.multiple_of(core * half, half), half)
+                both[g, b] = both[g, b] + part[g % 2, b, at, :]
+                return carry
+            lax.fori_loop(0, LAYERS, add, 0)
+            nearby(g, 1).start()
+            nearby(g, 0).start()
+    for g in range(groups):
+        nearby(g, 0).wait_recv()
+        away(g).wait_recv()
+        out_ref[g] = (both[g, layer] + near[g, 0]) + far[g]
+    for g in range(groups):
+        for d in range(1, PLANE):
+            swap(g, d).wait_send()
+        if g >= groups - 2:
+            cores(g).wait_send()
+        nearby(g, 0).wait_send()
+        nearby(g, 1).wait_send()
+        away(g).wait_send()
+
+
+def fast_cycle(amps, integrals, occ_limit, slot_order, col_ids):
     redist_count = lax.axis_size("redist")
-    occ_total = occ_irrep.shape[0]
-    slab = integrals.shape[2]
+    occ_total = occ_limit.shape[0]
+    share = amps.shape[2]
+    lanes = amps.shape[1]
+    slab, columns = integrals.shape[2:]
+    slot_dev = lanes // redist_count
+    per = redist_count
+    pair = amps.shape[0] // occ_total
+    groups = occ_total // per
+    rows = pair * share
+    full = slab * columns
+    depth = PLANE * rows
+    wide = LAYERS * lanes
+
+    me = lax.axis_index("redist")
+    layer, mate = me // PLANE, me % PLANE
+    mate_y, mate_x = mate // 2, mate % 2
+
+    chosen = (slot_order.reshape(LAYERS, PLANE, slot_dev)[None] ==
+              jnp.arange(lanes, dtype=jnp.int32)[:, None, None, None])
+    same = jnp.eye(LAYERS, dtype=jnp.bool_)
+    first = (chosen[None, :, :, None, :, :] & same[:, None, None, :, None, None])
+    first = first.reshape(wide, wide).astype(jnp.bfloat16)
+    old = jnp.arange(wide, dtype=jnp.int32)
+    target = ((old // slot_dev) % PLANE) * lanes + (old // (slot_dev * PLANE)) * slot_dev + old % slot_dev
+    second = (target[:, None] == old[None, :]).astype(jnp.bfloat16)
+
+    x = jnp.transpose(amps, (0, 2, 1)).reshape(pair, groups, per, share, lanes)
+    ordered = pl.pallas_call(
+        regroup_kernel,
+        grid=(groups,),
+        out_shape=jax.ShapeDtypeStruct((PLANE, groups, LAYERS, rows, lanes), jnp.float32),
+        in_specs=[
+            pl.BlockSpec((pair, 1, per, share, lanes), lambda g: (0, g, 0, 0, 0)),
+            pl.BlockSpec((wide, wide), lambda g: (0, 0)),
+            pl.BlockSpec((wide, wide), lambda g: (0, 0)),
+        ],
+        out_specs=pl.BlockSpec((PLANE, 1, LAYERS, rows, lanes), lambda g: (0, g, 0, 0, 0)),
+        compiler_params=pltpu.CompilerParams(vmem_limit_bytes=48 * 2**20),
+        name="regroup",
+    )(x, first, second)
+
+    slabs, limits = [], []
+    for d in range(PLANE):
+        mate_d = ((mate_y + d // 2) % 2) * 2 + (mate_x + d % 2) % 2
+        at = (layer * PLANE + mate_d) * pair
+        slabs.append(lax.dynamic_slice_in_dim(integrals, at, pair, 0))
+        limits.append(lax.dynamic_slice_in_dim(occ_limit, at, pair, 0))
+    w = jnp.concatenate(slabs, axis=0)
+    keep = col_ids[None, :] < jnp.concatenate(limits)[:, None]
+    w = jnp.where(keep[:, :, None, None], w, jnp.zeros((), w.dtype))
+    w = w.reshape(PLANE * pair, share, slab, 2, columns // 2)
+    w = jnp.transpose(w, (3, 2, 4, 0, 1)).reshape(full, depth)
+    w_top = lax.reduce_precision(w, 8, 7)
+    w_hi = w_top.astype(jnp.bfloat16)
+    w_lo = (w - w_top).astype(jnp.bfloat16)
+
+    vmem = pl.BlockSpec(memory_space=pltpu.VMEM)
+    dma = pltpu.SemaphoreType.DMA
+    out = pl.pallas_call(
+        cycle_kernel,
+        out_shape=jax.ShapeDtypeStruct((groups, full // 2, lanes), jnp.float32),
+        in_specs=[pl.BlockSpec(memory_space=pl.ANY), vmem, vmem],
+        out_specs=vmem,
+        scratch_shapes=[
+            pltpu.VMEM((groups, PLANE, LAYERS, rows, lanes), jnp.float32),
+            pltpu.VMEM((LAYERS, depth, lanes), jnp.bfloat16),
+            pltpu.VMEM((LAYERS, depth, lanes), jnp.bfloat16),
+            pltpu.VMEM((2, LAYERS, full, lanes), jnp.float32),
+            pltpu.VMEM((groups, LAYERS, full // 2, lanes), jnp.float32),
+            pltpu.VMEM((groups, 2, full // 2, lanes), jnp.float32),
+            pltpu.VMEM((groups, full // 2, lanes), jnp.float32),
+            dma((groups,)),
+            dma((groups, PLANE - 1)), dma((groups, PLANE - 1)),
+            dma((groups,)), dma((groups,)),
+            dma((groups, 2)), dma((groups, 2)),
+            dma((groups,)), dma((groups,)),
+        ],
+        compiler_params=pltpu.CompilerParams(
+            collective_id=0, has_side_effects=True, vmem_limit_bytes=60 * 2**20
+        ),
+        cost_estimate=pl.CostEstimate(
+            flops=6 * full * depth * groups * wide,
+            bytes_accessed=4 * depth * groups * wide,
+            transcendentals=0,
+        ),
+        name="cycle",
+    )(ordered, w_hi, w_lo)
+    out = out.reshape(groups, slab, columns // 2, per, slot_dev)
+    return jnp.transpose(out, (0, 3, 4, 1, 2)).reshape(occ_total, slot_dev, slab, columns // 2)
+
+
+def plain_cycle(amps, integrals, occ_limit, slot_order, col_ids):
+    redist_count = lax.axis_size("redist")
+    occ_total = occ_limit.shape[0]
     share = integrals.shape[1]
-    irrep_total = vir_energy.shape[0]
-    slot_total = vir_energy.shape[1]
-    slot_dev = slot_total // redist_count
-    labels = jnp.arange(irrep_total, dtype=jnp.int32)
-    hits = occ_irrep[:, None] == labels[None, :]
-    occ_limit = jnp.sum(jnp.where(hits, block_sizes[None, :], 0), axis=1)
+    slot_dev = slot_order.shape[0] // redist_count
     ordered = jnp.take(amps, slot_order, axis=1)
     moved = lax.all_to_all(ordered, "redist", split_axis=1, concat_axis=0, tiled=True)
     blocks = moved.reshape(occ_total, occ_total, slot_dev, share)
-    col_first = lax.axis_index("contract") * share
-    col_ids = col_first + jnp.arange(share, dtype=jnp.int32)
     keep_kc = col_ids[None, :] < occ_limit[:, None]
     masked = jnp.where(keep_kc[:, None, None, :], blocks, jnp.zeros((), blocks.dtype))
     summed = lax.psum_scatter(
@@ -34,11 +276,39 @@
         scatter_dimension=0,
         tiled=True,
     )
-    cycle = jnp.transpose(summed, (1, 2, 3, 0))
+    return jnp.transpose(summed, (1, 2, 3, 0))
+
+
+def per_device(amps, integrals, occ_irrep, block_sizes, slot_order, occ_energy, vir_energy):
+    redist_count = lax.axis_size("redist")
+    occ_total = occ_irrep.shape[0]
+    slab = integrals.shape[2]
+    share = integrals.shape[1]
+    irrep_total = vir_energy.shape[0]
+    slot_total = vir_energy.shape[1]
+    slot_dev = slot_total // redist_count
+    labels = jnp.arange(irrep_total, dtype=jnp.int32)
+    hits = occ_irrep[:, None] == labels[None, :]
+    occ_limit = jnp.sum(jnp.where(hits, block_sizes[None, :], 0), axis=1)
+    col_first = lax.axis_index("contract") * share
+    col_ids = col_first + jnp.arange(share, dtype=jnp.int32)
+    fits = (
+        redist_count == PLANE * LAYERS
+        and lax.axis_size("contract") == 2
+        and amps.shape[0] % occ_total == 0
+        and occ_total % redist_count == 0
+        and slot_total == 128
+        and slot_dev % 8 == 0
+    )
+    form = fast_cycle if fits else plain_cycle
+    cycle = form(amps, integrals, occ_limit, slot_order, col_ids)
     my_slots = lax.dynamic_slice_in_dim(
         slot_order, lax.axis_index("redist") * slot_dev, slot_dev, 0
     )
-    vir_rows = jnp.take(vir_energy, my_slots, axis=1)
+    mine = my_slots[:, None] == jnp.arange(slot_total, dtype=jnp.int32)[None, :]
+    vir_rows = jnp.sum(
+        jnp.where(mine[None], vir_energy[:, None, :], jnp.zeros((), vir_energy.dtype)), axis=2
+    )
     row_energy = jnp.sum(
         jnp.where(hits[:, :, None], vir_rows[None, :, :], jnp.zeros((), vir_rows.dtype)), axis=1
     )

time: 644 us -> 407 us (0.63)
  waiting for transfers between devices: 398 us -> 0 us
  Pallas kernels: 0 us -> 253 us
  matrix products: 118 us -> 0 us
  other arithmetic: 17 us -> 54.3 us
  between operations: 13.5 us -> 0.13 us
  local copies, waits for them, and re-layouts: 88.5 us -> 97.4 us
  starting transfers between devices: 7.45 us -> 0 us
    all_to_all x1 -> x0, waiting for transfers between devices: 336 us -> none  [per_device(): lax.all_to_all(ordered, 'redist', split_axis=1, concat_axis=0, tiled=True)]
    pallas_call x0 -> x2, Pallas kernels: none -> 253 us  [the longest x1 235 us: fast_cycle(): pl.pallas_call(cycle_kernel, out_shape=jax.ShapeDtypeStruct((groups, full...]
    dot_general x1 -> x0, matrix products: 118 us -> none  [per_device(): jnp.einsum('kiac,kcjb->biaj', masked, integrals, precision=lax.Precision....]
    reduce_scatter x1 -> x0, waiting for transfers between devices: 61.7 us -> none  [per_device(): lax.psum_scatter(jnp.einsum('kiac,kcjb->biaj', masked, integrals, precisi...]
    transpose x0 -> x1, other arithmetic: none -> 35.5 us  [fast_cycle(): w = jnp.transpose(w, (3, 2, 4, 0, 1)).reshape(full, depth)]
    reshape x1 -> x3, local copies, waits for them, and re-layouts: 24.2 us -> 57.7 us  [the longest x2 54.6 us: fast_cycle(): w = jnp.transpose(w, (3, 2, 4, 0, 1)).reshape(full, depth)]
    concatenate x0 -> x4, local copies, waits for them, and re-layouts: none -> 23 us  [fast_cycle(): w = jnp.concatenate(slabs, axis=0)]
    all_to_all x1 -> x0, local copies, waits for them, and re-layouts: 17.8 us -> none  [per_device(): lax.all_to_all(ordered, 'redist', split_axis=1, concat_axis=0, tiled=True)]
  transfers between devices with their start and end apart: 2 -> 0, of which waited for: 2 -> 0; matrix products, arithmetic and copies ran while one was open for 0% -> 0% of each run, Pallas kernels for 0% -> 0%
where the time goes in v1:
time: 407 us; the launch traced here: 405 us
  Pallas kernels  253 us (62%)
  local copies, waits for them, and re-layouts  97.4 us (24%)
  other arithmetic  54.3 us (13%)
    pallas_call x1, Pallas kernels, fast_cycle(): pl.pallas_call(cycle_kernel, out_shape=jax.ShapeDtypeStruct((groups, full...  235 us
    reshape x2, local copies, waits for them, and re-layouts, fast_cycle(): w = jnp.transpose(w, (3, 2, 4, 0, 1)).reshape(full, depth)  54.6 us
    transpose x1, other arithmetic, fast_cycle(): w = jnp.transpose(w, (3, 2, 4, 0, 1)).reshape(full, depth)  35.5 us
    concatenate x4, local copies, waits for them, and re-layouts, fast_cycle(): w = jnp.concatenate(slabs, axis=0)  23 us
    pallas_call x1, Pallas kernels, fast_cycle(): pl.pallas_call(regroup_kernel, grid=(groups,), out_shape=jax.ShapeDtypeSt...  18 us
    convert_element_type x1, other arithmetic, fast_cycle(): w_lo = (w - w_top).astype(jnp.bfloat16)  9.39 us

profile of v1, /device:TPU:4, one launch (start us, length us, event | category | flops | bytes accessed | tf_op | source)
XLA Modules:
  0.0 404.9 jit_solution(1339319842247974600)
XLA Ops:
  0.0 0.8 select_reduce_fusion.3
  0.8 0.1 fusion.17
  0.8 0.1 pad_add_fusion
  0.9 0.1 broadcast_compare_fusion.1
  1.0 7.6 %constant_dynamic-slice_fusion.4 = (f32[5,64,16,128]{3,2,1,0:T(8,128)}, f32[5,64,16,128]{3,2,1,0:T(8,128)}, f32[5,64,16,128]{3,2,1,0:T(8,128)S(1)}, f32[5,64,16,128]{3,2,1,0:T(8,128)}) fusion(f32[80,64,16,128]{3,2,1,0:T(8,128)} %param.8, s32[]{:T(128)S(6)} %select_n.135, s32[]{:T(128)S(6)} %select_n.137, s32[]{:T(128)S(6)} %select_n.140, s32[]{:T(128)S(6)} %select_n.139), kind=kLoop, calls=%fused_computation.49 | loop fusion | bytes 20971536 | tf_op jit(solution)/shard_map/dynamic_slice | solution.py:211
  8.6 6.2 %concatenate.16 = f32[5,64,16,2,64]{4,3,2,1,0:T(2,128)} reshape(f32[5,64,16,128]{3,2,1,0:T(8,128)} %get-tuple-element.5) | data formatting | bytes 5242880 | tf_op jit(solution)/shard_map/concatenate | solution.py:213
  14.8 6.2 %concatenate.17 = f32[5,64,16,2,64]{4,3,2,1,0:T(2,128)} reshape(f32[5,64,16,128]{3,2,1,0:T(8,128)} %get-tuple-element.6) | data formatting | bytes 5242880 | tf_op jit(solution)/shard_map/concatenate | solution.py:213
  21.0 6.2 %concatenate.18 = f32[5,64,16,2,64]{4,3,2,1,0:T(2,128)} reshape(f32[5,64,16,128]{3,2,1,0:T(8,128)} %get-tuple-element.8) | data formatting | bytes 5242880 | tf_op jit(solution)/shard_map/concatenate | solution.py:213
  27.2 4.4 %concatenate.19 = f32[5,64,16,2,64]{4,3,2,1,0:T(2,128)} reshape(f32[5,64,16,128]{3,2,1,0:T(8,128)S(1)} %get-tuple-element.7) | data formatting | bytes 5242880 | tf_op jit(solution)/shard_map/concatenate | solution.py:213
  31.5 35.5 %fusion = f32[2,16,64,20,64]{2,0,1,4,3:T(2,128)} fusion(f32[5,64,16,2,64]{4,3,2,1,0:T(2,128)} %concatenate.19, f32[5,64,16,2,64]{4,3,2,1,0:T(2,128)} %concatenate.18, f32[5,64,16,2,64]{4,3,2,1,0:T(2,128)} %concatenate.17, f32[5,64,16,2,64]{4,3,2,1,0:T(2,128)} %concatenate.16, pred[20,64]{1,0:T(8,128)(4,1)S(1)} %broadcast_compare_fusion.1), kind=kLoop, calls=%fused_computation.1 | loop fusion | flops 10485760 | bytes 20972800 | tf_op jit(solution)/shard_map/transpose | solution.py:217
  67.0 35.7 %copy.23 = f32[2,16,64,20,64]{4,3,2,1,0:T(8,128)} copy(f32[2,16,64,20,64]{2,0,1,4,3:T(2,128)} %fusion) | data formatting | bytes 20971520 | tf_op jit(solution)/shard_map/reshape | solution.py:217
  102.7 18.9 %reshape.214 = f32[2048,1280]{1,0:T(8,128)} reshape(f32[2,16,64,20,64]{4,3,2,1,0:T(8,128)} %copy.23) | data formatting | bytes 20971520 | tf_op jit(solution)/shard_map/reshape | solution.py:217
  121.6 0.0 copy-start.2
  121.6 9.4 %fusion.1 = (bf16[2048,1280]{1,0:T(8,128)(2,1)}, bf16[2048,1280]{1,0:T(8,128)(2,1)}) fusion(f32[2048,1280]{1,0:T(8,128)} %reshape.214), kind=kLoop, calls=%fused_computation.4 | loop fusion | flops 10485760 | bytes 20971520 | tf_op jit(solution)/shard_map/convert_element_type | solution.py:220
  131.0 0.0 copy-done.2
  131.0 0.1 eq.90
  131.1 0.1 iota_compare_fusion.1
  131.2 0.3 and_convert_fusion
  131.6 0.1 copy.27
  131.7 0.2 copy.15.first_ref
  131.9 0.2 fusion.3.second_ref
  132.1 18.0 %regroup.1.a_ref = f32[4,5,4,320,128]{4,3,2,1,0:T(8,128)} custom-call(f32[5,5,16,64,128]{4,3,2,1,0:T(8,128)} %bitcast.31, bf16[512,512]{1,0:T(8,128)(2,1)S(1)} %copy.15.first_ref, bf16[512,512]{1,0:T(8,128)(2,1)S(1)} %fusion.3.second_ref), custom_call_target="tpu_custom_call" | custom-call | tf_op jit(solution)/shard_map/regroup/pallas_call | solution.py:193
  150.1 235.0 %cycle.1 = f32[5,1024,128]{2,1,0:T(8,128)} custom-call(f32[4,5,4,320,128]{4,3,2,1,0:T(8,128)} %regroup.1.a_ref, bf16[2048,1280]{1,0:T(8,128)(2,1)} %get-tuple-element.10.hi_ref, bf16[2048,1280]{1,0:T(8,128)(2,1)} %get-tuple-element.9.lo_ref), custom_call_target="tpu_custom_call" | custom-call | flops 40265318400 | bytes 13107200 | tf_op jit(solution)/shard_map/cycle/pallas_call | solution.py:224
  385.1 2.2 copy.19
  387.2 0.0 copy-start
  387.3 0.0 copy-start.3
  387.3 0.0 copy-start.1
  387.3 3.0 reshape.211
  390.3 0.1 dynamic_slice.30
  390.4 0.1 broadcast_compare_fusion
  390.5 0.1 iota_compare_fusion.2
  390.6 0.0 copy-done
  390.6 0.1 select_reduce_fusion.2
  390.6 0.0 copy-done.3
  390.7 0.1 select_reduce_fusion.1
  390.7 0.1 copy.20
  390.8 0.1 constant_dynamic-slice_fusion
  390.9 0.1 copy.21
  391.0 0.1 select_reduce_fusion
  391.1 0.1 broadcast_compare_fusion.2
  391.2 0.0 copy-done.1
  391.2 7.5 %fusion.2 = f32[80,8,16,64]{3,2,1,0:T(8,128)} fusion(f32[5,16,64,16,8]{2,1,4,3,0:T(8,128)} %reshape.211, f32[16]{0:T(128)S(1)} %bitcast.36, f32[80]{0:T(128)S(1)} %copy-done.1, f32[16,64]{1,0:T(8,128)S(1)} %select_reduce_fusion, f32[80,8]{1,0:T(8,128)S(1)} %copy.20, pred[16,64]{1,0:T(8,128)(4,1)S(1)} %broadcast_compare_fusion.2, ...), kind=kLoop, calls=%fused_computation.6 | loop fusion | flops 3932160 | bytes 5251584 | tf_op jit(solution)/shard_map/jit(_where)/select_n | solution.py:328
  398.6 6.3 %copy.22 = f32[80,8,16,64]{0,3,2,1:T(8,128)} copy(f32[80,8,16,64]{3,2,1,0:T(8,128)} %fusion.2) | data formatting | bytes 5242880 | tf_op jit(solution)/shard_map/jit(_where)/select_n | solution.py:328
  (4 shorter events, 0.0 us)
Async XLA Ops:
  121.6 9.4 %copy-start.2 = (s32[128]{0:T(128)S(1)}, s32[128]{0:T(128)}, u32[]{:S(2)}) copy-start(s32[128]{0:T(128)} %param.11) | copy-start | bytes 1540
  387.2 3.3 copy-start
  387.3 3.4 copy-start.3
  387.3 3.9 copy-start.1
